TPU v7x, 256 devices: a whole 4x4x8 slice. The times are simulated.
256 devices in a mesh: grp: 16 (over z_lo, y, core), ctx: 16 (over x, z_hi).
Axes of the slice: x: 4, y: 4, z: 8 (z_hi: 4, z_lo: 2; z = z_hi * 2 + z_lo), core: 2. Of those that a mesh axis runs over, the one named last changes fastest.
Arguments:
- history: bfloat16 [16, 3072, 1024], P('grp', 'ctx'), may hold values from -6 to 6
- candidates: bfloat16 [16, 4096, 1024], P('grp', 'ctx'), may hold values from -6 to 6
- lengths: int32 [16], P('grp'), may hold values from 768 to 3072, as said below
- block_order: int32 [16, 16], P('grp'), may hold values from 0 to 15, each once within a row
- targets: int32 [16, 4096], P('grp', 'ctx'), may hold values from 0 to 7
- projection: bfloat16 [1024, 4096], replicated, may hold values from -0.1875 to 0.1875
- output_weight: bfloat16 [1024, 1024], P('grp'), may hold values from -0.1875 to 0.1875
- task_weight: bfloat16 [1024, 8], replicated, may hold values from -0.1875 to 0.1875
Outputs:
- layer_output: bfloat16 [16, 3072, 1024], P('grp', 'ctx')
- task_logprob: float32 [16, 4096], P('grp', 'ctx')
Inputs may be any that keep to these rules, and one draw needn't show every extreme that they name: `lengths`: each user's history holds 3072 stored rows, the live ones being positions below its length; some user has all 3072 live. `block_order`: each row is a permutation of 0 to 16 - 1.
All inputs are finite; a program needn't handle non-finite values.
Results may differ from a plain program's by a relative error of at most 0.005.
Values may be sent and summed in bfloat16 or wider, within the bound.
A program may use at most 128 MiB of HBM per device.

v0:
```python
import jax
import jax.numpy as jnp
from jax import lax
from jax.sharding import PartitionSpec as P

HEADS = 8


norm_eps = 1e-05


def layer_norm(mixed):
    centre = mixed - jnp.mean(mixed, axis=-1, keepdims=True)
    spread = jnp.mean(centre * centre, axis=-1, keepdims=True)
    return centre * lax.rsqrt(spread + norm_eps)


def block_positions(order_row, first_row, count, block_rows):
    stored = first_row + jnp.arange(count, dtype=jnp.int32)
    owner = stored // block_rows
    slots = jnp.arange(order_row.shape[0], dtype=jnp.int32)
    block_index = jnp.sum(
        jnp.where(owner[:, None] == slots[None, :], order_row[None, :], 0), axis=1
    )
    return block_index * block_rows + stored % block_rows


def attend(queries, keys, values, allowed):
    query_rows = queries.shape[0]
    key_rows = keys.shape[0]
    scale = (queries.shape[1] // HEADS) ** (-0.5)
    query_heads = queries.reshape(query_rows, HEADS, -1)
    key_heads = keys.reshape(key_rows, HEADS, -1)
    value_heads = values.reshape(key_rows, HEADS, -1)
    scores = (
        jnp.einsum("qhd,khd->hqk", query_heads, key_heads, preferred_element_type=jnp.float32)
        * scale
    )
    weights = jnp.where(allowed[None], jax.nn.silu(scores), 0.0).astype(jnp.bfloat16)
    mixed = jnp.einsum("hqk,khd->qhd", weights, value_heads, preferred_element_type=jnp.float32)
    return mixed.reshape(query_rows, -1)


def self_mix(queries, keys, values):
    count = queries.shape[0]
    scale = (queries.shape[1] // HEADS) ** (-0.5)
    head_scores = (
        jnp.sum(
            (queries.astype(jnp.float32) * keys.astype(jnp.float32)).reshape(count, HEADS, -1),
            axis=-1,
        )
        * scale
    )
    weights = jax.nn.silu(head_scores).astype(jnp.bfloat16)
    weights = lax.optimization_barrier(weights).astype(jnp.float32)
    return (weights[:, :, None] * values.astype(jnp.float32).reshape(count, HEADS, -1)).reshape(
        count, -1
    )


def local(
    history, candidates, lengths, block_order, targets, projection, output_weight, task_weight
):
    hist_rows = history.shape[1]
    cand_rows = candidates.shape[1]
    width = history.shape[2]
    order_row = block_order[0]
    limit = lengths[0]
    query_pos = block_positions(order_row, lax.axis_index("ctx") * hist_rows, hist_rows, hist_rows)
    stacked = jnp.concatenate([history[0], candidates[0]], axis=0)
    projected = jax.nn.silu(
        jnp.dot(stacked, projection, preferred_element_type=jnp.float32)
    ).astype(jnp.bfloat16)
    gates = projected[:, :width]
    values = projected[:, width : 2 * width]
    queries = projected[:, 2 * width : 3 * width]
    keys = projected[:, 3 * width :]
    hist_query = queries[:hist_rows]
    cand_query = queries[hist_rows:]
    hist_keys = keys[:hist_rows]
    hist_values = values[:hist_rows]
    pieces = (
        lax.all_gather(hist_keys, "ctx", axis=0, tiled=True),
        lax.all_gather(hist_values, "ctx", axis=0, tiled=True),
    )
    first_row = jnp.int32(0)
    key_pos = block_positions(order_row, first_row, pieces[0].shape[0], hist_rows)
    allowed = (key_pos[None, :] <= query_pos[:, None]) & (key_pos[None, :] < limit)
    hist_mix = attend(hist_query, pieces[0], pieces[1], allowed)
    piece_rows = pieces[0].shape[0]
    key_pos = block_positions(order_row, first_row, piece_rows, hist_rows)
    allowed = jnp.broadcast_to((key_pos < limit)[None, :], (cand_rows, piece_rows))
    cand_mix = attend(cand_query, pieces[0], pieces[1], allowed)
    cand_mix = cand_mix + self_mix(cand_query, keys[hist_rows:], values[hist_rows:])
    mixed_rows = jnp.concatenate([hist_mix, cand_mix], axis=0)
    gated = (layer_norm(mixed_rows) * gates.astype(jnp.float32)).astype(jnp.bfloat16)
    branch = jnp.dot(
        gated,
        lax.all_gather(output_weight, "grp", axis=0, tiled=True),
        preferred_element_type=jnp.float32,
    )
    hist_out = history[0].astype(jnp.float32) + branch[:hist_rows]
    hist_out = jnp.where((query_pos < limit)[:, None], hist_out, 0.0).astype(jnp.bfloat16)
    cand_out = (candidates[0].astype(jnp.float32) + branch[hist_rows:]).astype(jnp.bfloat16)
    logits = jnp.dot(cand_out, task_weight, preferred_element_type=jnp.float32)
    task_ids = jnp.arange(task_weight.shape[1], dtype=jnp.int32)
    picked = jnp.sum(jnp.where(targets[0][:, None] == task_ids[None, :], logits, 0.0), axis=1)
    return (hist_out[None], (-jax.nn.softplus(-picked))[None])


def solution(mesh):
    in_specs = (
        P("grp", "ctx", None),
        P("grp", "ctx", None),
        P("grp"),
        P("grp", None),
        P("grp", "ctx"),
        P(),
        P("grp", None),
        P(),
    )
    out_specs = (P("grp", "ctx", None), P("grp", "ctx"))
    return jax.shard_map(local, mesh=mesh, in_specs=in_specs, out_specs=out_specs, check_vma=False)
```

profile of v0, /device:TPU:1, one launch (start us, length us, event | category | flops | bytes accessed | tf_op | source)
XLA Modules:
  0.0 267.0 jit_solution(8494888255223471933)
XLA Ops:
  7.2 8.4 %multiply_convert_fusion = bf16[448,4096]{1,0:T(8,128)(2,1)S(1)} fusion(bf16[1024,4096]{1,0:T(8,128)(2,1)} %param.13, bf16[256,1024]{1,0:T(8,128)(2,1)} %bitcast.82, bf16[192,1024]{1,0:T(8,128)(2,1)} %bitcast.83), kind=kOutput, calls=%fused_computation.5 | convolution fusion | flops 3769106432 | bytes 12976128 | tf_op jit(solution)/shard_map/dot_general | solution.py:72
  15.7 1.8 copy-done.1
  17.5 1.0 slice_bitcast_fusion.1
  18.6 0.7 all-gather.6.cloned.1.call-update
  19.3 0.2 all-gather.8.cloned.1.call-start
  19.5 0.5 all-gather.8.cloned.1.call-update
  20.0 1.4 multiply_bitcast_fusion
  22.3 0.2 copy.51
  22.5 0.3 reduce_sum.60
  23.1 0.5 compare_and_fusion
  23.6 89.7 %all-gather.4.cloned.1.call-done = bf16[3072,1024]{1,0:T(8,128)(2,1)} async-done(((bf16[192,1024]{1,0:T(8,128)(2,1)}), bf16[3072,1024]{1,0:T(8,128)(2,1)}) %all-gather.4.cloned.1.call-update) | async-done | bytes 6291472 | tf_op jit(solution)/shard_map/all_gather | solution.py:84
  113.2 8.7 %copy.46 = bf16[3072,1024]{0,1:T(8,128)(2,1)} copy(bf16[3072,1024]{1,0:T(8,128)(2,1)} %all-gather.4.cloned.1.call-done) | data formatting | bytes 12582912 | tf_op jit(solution)/shard_map/reshape | solution.py:34
  122.0 90.0 %all-gather.6.cloned.1.call-done = bf16[3072,1024]{1,0:T(8,128)(2,1)} async-done(((bf16[192,1024]{1,0:T(8,128)(2,1)}), bf16[3072,1024]{1,0:T(8,128)(2,1)}) %all-gather.6.cloned.1.call-update) | async-done | bytes 6291472 | tf_op jit(solution)/shard_map/all_gather | solution.py:83
  211.9 11.7 %fusion.15 = f32[8,24,8,128]{3,2,1,0:T(8,128)S(1)} fusion(bf16[3072,8,128]{0,2,1:T(8,128)(2,1)} %bitcast.77, pred[192,3072]{1,0:T(8,128)(4,1)S(1)} %compare_and_fusion, bf16[24,8,8,128]{3,2,1,0:T(8,128)(2,1)S(1)} %get-tuple-element.4, bf16[3072,1024]{1,0:T(8,128)(2,1)} %all-gather.6.cloned.1.call-done), kind=kOutput, calls=%fused_computation.15 | convolution fusion | flops 2448949248 | bytes 14352384 | tf_op jit(solution)/shard_map/hqk,khd->qhd/dot_general | solution.py:40
  223.7 15.3 %fusion = f32[8,128,256]{2,1,0:T(8,128)S(1)} fusion(bf16[3072,8,128]{0,2,1:T(8,128)(2,1)} %bitcast.78, pred[3072]{0:T(1024)(128)(4,1)S(1)} %broadcast_compare_fusion, bf16[3072,1024]{1,0:T(8,128)(2,1)} %all-gather.6.cloned.1.call-done, bf16[448,4096]{1,0:T(8,128)(2,1)} %copy-done.1), kind=kOutput, calls=%fused_computation.2 | convolution fusion | flops 3265265664 | bytes 14158848 | tf_op jit(solution)/shard_map/hqk,khd->qhd/dot_general | solution.py:40
  239.0 0.3 copy.45
  239.4 0.3 mul.101
  239.7 1.5 fusion.20
  241.4 0.3 multiply_reduce_fusion
  241.7 13.9 %all-gather.8.cloned.1.call-done = bf16[1024,1024]{1,0:T(8,128)(2,1)} async-done(((bf16[64,1024]{1,0:T(8,128)(2,1)}), bf16[1024,1024]{1,0:T(8,128)(2,1)}) %all-gather.8.cloned.1.call-update) | async-done | bytes 2097168 | tf_op jit(solution)/shard_map/all_gather | solution.py:99
  255.6 3.1 %fusion.22 = f32[448,1024]{1,0:T(8,128)S(1)} fusion(bf16[1024,1024]{1,0:T(8,128)(2,1)} %all-gather.8.cloned.1.call-done, f32[256,1024]{1,0:T(8,128)S(1)} %fusion.20, f32[192,1024]{1,0:T(8,128)S(1)} %bitcast.76, bf16[448,4096]{1,0:T(8,128)(2,1)} %copy-done.1, f32[448]{0:T(512)S(1)} %add_rsqrt_fusion, f32[448]{0:T(512)S(1)} %broadcast_multiply_fusion), kind=kOutput, calls=%fused_computation.24 | convolution fusion | flops 942276608 | bytes 6688256 | tf_op jit(solution)/shard_map/dot_general | solution.py:97
  258.7 0.9 fusion.39
  259.6 0.3 fusion.19
  259.9 0.6 fusion.53
  (29 shorter events, 0.8 us)
Async XLA Ops:
  7.2 252.4 %copy-start = (bf16[1024,8]{0,1:T(8,128)(2,1)S(1)}, bf16[1024,8]{0,1:T(8,128)(2,1)}, u32[]{:S(2)}) copy-start(bf16[1024,8]{0,1:T(8,128)(2,1)} %param.15) | copy-start | bytes 49156
  7.2 106.1 %all-gather.4.cloned.1.call-start = ((), (), s32[]{:S(2)}) async-start(), calls=%async_computation | async-start | bytes 6684672 | tf_op jit(solution)/shard_map/all_gather | solution.py:84
  7.2 14.9 %copy-start.4 = (s32[1,16]{1,0:T(1,128)S(1)}, s32[1,16]{1,0:T(1,128)}, u32[]{:S(2)}) copy-start(s32[1,16]{1,0:T(1,128)} %param.11) | copy-start | bytes 196
  15.7 1.9 copy-start.1
  18.5 193.4 %all-gather.6.cloned.1.call-start = ((), (), s32[]{:S(2)}) async-start(), calls=%async_computation.1 | async-start | bytes 6684672 | tf_op jit(solution)/shard_map/all_gather | solution.py:83
  19.3 236.3 %all-gather.8.cloned.1.call-start = ((), (), s32[]{:S(2)}) async-start(), calls=%async_computation.2 | async-start | bytes 2228224 | tf_op jit(solution)/shard_map/all_gather | solution.py:99
  241.7 17.0 %copy-start.3 = (bf16[1,192,1024]{2,1,0:T(8,128)(2,1)S(1)}, bf16[1,192,1024]{2,1,0:T(8,128)(2,1)}, u32[]{:S(2)}) copy-start(bf16[1,192,1024]{2,1,0:T(8,128)(2,1)} %param.8) | copy-start | bytes 1179652
  241.7 17.9 %copy-start.2 = (bf16[1,256,1024]{2,1,0:T(8,128)(2,1)S(1)}, bf16[1,256,1024]{2,1,0:T(8,128)(2,1)}, u32[]{:S(2)}) copy-start(bf16[1,256,1024]{2,1,0:T(8,128)(2,1)} %param.9) | copy-start | bytes 1572868
  241.7 17.9 %copy-start.5 = (s32[1,256]{1,0:T(1,128)S(1)}, s32[1,256]{1,0:T(1,128)}, u32[]{:S(2)}) copy-start(s32[1,256]{1,0:T(1,128)} %param.12) | copy-start | bytes 3076
Sparse Core Ops, SparseCore 0:
  18.6 94.5 all-gather.3
  116.3 95.5 all-gather.5
  213.8 41.7 all-gather.7
where the time goes:
time: 267 us
  waiting for transfers between devices  195 us (73%)
  matrix products  38.8 us (15%)
  between operations  14.6 us (5%)
  local copies, waits for them, and re-layouts  12.7 us (5%)
  other arithmetic  5.89 us (2%)
    all_gather x1, waiting for transfers between devices, local(): lax.all_gather(hist_keys, 'ctx', axis=0, tiled=True)  90 us
    all_gather x1, waiting for transfers between devices, local(): lax.all_gather(hist_values, 'ctx', axis=0, tiled=True)  89.7 us
    dot_general x2, matrix products, attend(): jnp.einsum('hqk,khd->qhd', weights, value_heads, preferred_element_type=j...  27 us
    all_gather x1, waiting for transfers between devices, local(): lax.all_gather(output_weight, 'grp', axis=0, tiled=True)  13.9 us
    reshape x1, local copies, waits for them, and re-layouts, attend(): value_heads = values.reshape(key_rows, HEADS, -1)  8.71 us
    dot_general x1, matrix products, local(): jnp.dot(stacked, projection, preferred_element_type=jnp.float32)  8.41 us
  transfers between devices with their start and end apart: 3, of which 3 were waited for; matrix products, arithmetic and copies ran while one was open for 15% of the time, Pallas kernels for 0%

commit v1 on v0

v1 whole, which is shorter than its diff:
```python
import functools

import jax
import jax.numpy as jnp
from jax import lax
from jax.experimental import pallas as pl
from jax.experimental.pallas import tpu as pltpu
from jax.sharding import PartitionSpec as P

HEADS = 8
NORM_EPS = 1e-05
ROUNDS = 6
F32, BF16 = jnp.float32, jnp.bfloat16
MESH = pl.DeviceIdType.MESH


def silu_of_double(half):
    return half + half * jnp.tanh(half)


def layer_norm(mixed):
    centre = mixed - jnp.mean(mixed, axis=-1, keepdims=True)
    spread = jnp.mean(centre * centre, axis=-1, keepdims=True)
    return centre * lax.rsqrt(spread + NORM_EPS)


def kernel(
    hist, cand, lengths, order, proj, out_weight, task_t,
    hist_out, logits_out,
    w, ow, hb, cb, xb, kv, pj, acc, gated, stage, mloc, mb, lbuf,
    w_sem, hb_send, hb_recv, cb_send, cb_recv, mb_send, mb_recv,
    h_send, h_recv, z_send, z_recv, e_send, e_recv, d_send, d_recv,
    ow_send, ow_recv, ow_local, ret_send, ret_recv,
):
    rows = hb.shape[0]
    cands = cb.shape[0]
    width = hb.shape[1]
    part = rows // ROUNDS
    half = part // 2
    column = 4 * part
    mine = 2 * column
    head = width // HEADS
    half_scale = 0.5 * head ** (-0.5)

    g = lax.axis_index("grp")
    c = lax.axis_index("ctx")
    core = lax.rem(g, 2)
    pair = g - core
    zlo = g // 8
    y = lax.rem(g // 2, 4)
    x = c // 4
    z = lax.rem(c, 4)
    swapped = lax.rem(x // 2 + core, 2)
    home_core = lax.rem(core + swapped, 2)
    home_x = x + swapped * (3 - 2 * x)
    z_up = lax.rem(z + 1, 4)
    z_down = lax.rem(z + 3, 4)
    z_far = lax.rem(z + 2, 4)

    swap = (pair + home_core, home_x * 4 + z)
    home_up = (pair + home_core, home_x * 4 + z_up)
    home_down = (pair + home_core, home_x * 4 + z_down)
    col_up = (g, x * 4 + z_up)
    col_down = (g, x * 4 + z_down)
    across = (g, (x + 1 - 2 * lax.rem(x, 2)) * 4 + z)
    sibling = (pair + 1 - core, c)
    z_pair = ((1 - zlo) * 8 + y * 2 + core, c)
    y_others = [(zlo * 8 + lax.rem(y + i, 4) * 2 + core, c) for i in (1, 2, 3)]

    def remote(src, dst, send, recv, to):
        return pltpu.make_async_remote_copy(
            src_ref=src, dst_ref=dst, send_sem=send, recv_sem=recv, device_id=to, device_id_type=MESH
        )

    def arrived(ref, sem):
        pltpu.make_async_copy(ref, ref, sem).wait()

    barrier = pltpu.get_barrier_semaphore()
    greeted = [home_up, home_down, across, sibling, z_pair, *y_others]
    for other in greeted:
        pl.semaphore_signal(barrier, inc=1, device_id=other, device_id_type=MESH)

    @pl.when(swapped == 1)
    def _():
        pl.semaphore_signal(barrier, inc=1, device_id=swap, device_id_type=MESH)
        pl.semaphore_signal(barrier, inc=1, device_id=col_up, device_id_type=MESH)
        pl.semaphore_signal(barrier, inc=1, device_id=col_down, device_id_type=MESH)

    w_copy = pltpu.make_async_copy(proj, w, w_sem)
    w_copy.start()
    ow_own = pltpu.make_async_copy(out_weight, ow.at[zlo * 4 + y, core], ow_local)
    ow_own.start()

    lane = lax.broadcasted_iota(jnp.int32, (8, 2 * mine), 1)
    slot = lane // part
    own_block = order[0, c]
    limit = lengths[0]
    block = jnp.zeros_like(lane)
    x_pair = x + 1 - 2 * lax.rem(x, 2)
    columns = (x, x_pair, 3 - x, 3 - x_pair)
    for i, source in enumerate(columns):
        for zs in range(4):
            block = jnp.where(slot == 4 * i + zs, order[0, source * 4 + zs], block)
    row_id = lax.broadcasted_iota(jnp.int32, (8, 2 * mine), 0)
    first = block * rows + lax.rem(lane, part)
    causal = jnp.where(row_id == 0, block, -1) < own_block
    for r in range(ROUNDS):
        live = first + r * part < limit
        mloc[r] = jnp.where(live & causal, half_scale, 0.0)

    pl.semaphore_wait(barrier, len(greeted) + 3 * swapped)

    def hist_part(r):
        return hist.at[0, pl.ds(pl.multiple_of(r * part, part), part)]

    def slot_of(zs):
        return pl.ds(pl.multiple_of(zs * part, part), part)

    def send_up(r):
        return remote(hist_part(r), xb.at[r, 0, slot_of(z)], h_send.at[r, 0], h_recv.at[r, 0], home_up)

    def send_down(r):
        return remote(hist_part(r), xb.at[r, 0, slot_of(z)], h_send.at[r, 1], h_recv.at[r, 1], home_down)

    hb_remote = remote(hist.at[0], hb, hb_send, hb_recv, swap)
    cb_remote = remote(cand.at[0], cb, cb_send, cb_recv, swap)
    mb_remote = remote(mloc, mb, mb_send, mb_recv, swap)

    @pl.when(swapped == 1)
    def _():
        hb_remote.start()
        cb_remote.start()
        mb_remote.start()

    @pl.when(swapped == 0)
    def _():
        pltpu.make_async_copy(hist.at[0], hb, hb_recv).start()
        pltpu.make_async_copy(cand.at[0], cb, cb_recv).start()
        pltpu.make_async_copy(mloc, mb, mb_recv).start()

    @pl.loop(0, ROUNDS)
    def _(r):
        send_up(r).start()
        send_down(r).start()

    ow_mine = out_weight
    ow_slot = ow.at[zlo * 4 + y, core]
    ow_first = [remote(ow_mine, ow_slot, ow_send.at[0], ow_recv.at[0], z_pair)]
    for i in range(3):
        ow_first.append(remote(ow_mine, ow_slot, ow_send.at[1 + i], ow_recv.at[1 + i], y_others[i]))
    for copy in ow_first:
        copy.start()

    def ow_from(zl, yy):
        return ow.at[zl * 4 + yy, core]

    ow_other = ow_from(1 - zlo, y)
    ow_second = [
        remote(ow_other, ow_other, ow_send.at[4 + i], ow_recv.at[4 + i], y_others[i]) for i in range(3)
    ]
    ow_third = remote(ow.at[:, core], ow.at[:, core], ow_send.at[7], ow_recv.at[7], sibling)

    def own_part(r):
        return hb.at[pl.ds(pl.multiple_of(r * part, part), part)]

    def give(r, k, src, zs):
        return remote(src, xb.at[r, 1, slot_of(zs)], e_send.at[r, k], e_recv.at[r, k], across)

    def give_own(r):
        return give(r, 0, own_part(r), z)

    def give_down(r):
        return give(r, 1, xb.at[r, 0, slot_of(z_down)], z_down)

    def give_up(r):
        return give(r, 2, xb.at[r, 0, slot_of(z_up)], z_up)

    def give_far(r):
        return give(r, 3, xb.at[r, 0, slot_of(z_far)], z_far)

    def half_of(zs, i):
        return pl.ds(pl.multiple_of(zs * part + i * half, half), half)

    def pass_up(r):
        ref = xb.at[r, 0, half_of(z_down, 0)]
        return remote(ref, ref, z_send.at[r, 0], z_recv.at[r, 0], col_up)

    def pass_down(r):
        ref = xb.at[r, 0, half_of(z_up, 1)]
        return remote(ref, ref, z_send.at[r, 1], z_recv.at[r, 1], col_down)

    def near_blocks(r):
        arrived(xb.at[r, 0, slot_of(z_down)], h_recv.at[r, 0])
        pass_up(r).start()
        give_down(r).start()
        arrived(xb.at[r, 0, slot_of(z_up)], h_recv.at[r, 1])
        pass_down(r).start()
        give_up(r).start()

    def far_block(r):
        arrived(xb.at[r, 0, half_of(z_far, 0)], z_recv.at[r, 0])
        arrived(xb.at[r, 0, half_of(z_far, 1)], z_recv.at[r, 1])
        give_far(r).start()

    def share(r):
        return remote(kv.at[r, 0], kv.at[r, 1], d_send.at[r], d_recv.at[r], sibling)

    def project(src, base, count):
        for j in range(0, 4 * width, 256):
            p = jnp.dot(src[...], w[:, j : j + 256], preferred_element_type=F32)
            pj[base : base + count, j : j + 256] = silu_of_double(0.5 * p).astype(BF16)

    def keys_values(r):
        for k, zs in enumerate((z, z_down, z_up, z_far)):
            arrived(xb.at[r, 1, slot_of(zs)], e_recv.at[r, k])
        block_rows = xb[r].reshape(mine, width)
        for j in range(0, 2 * width, 256):
            start = width + j if j < width else 2 * width + j
            p = jnp.dot(block_rows, w[:, start : start + 256], preferred_element_type=F32)
            kv[r, 0, :, j : j + 256] = silu_of_double(0.5 * p).astype(BF16)
        share(r).start()

    def attend(r, base, count, mask_row):
        for h in range(HEADS):
            cols = slice(h * head, (h + 1) * head)
            key_cols = slice(width + h * head, width + (h + 1) * head)
            keys = kv[r, :, :, key_cols].reshape(2 * mine, head)
            values = kv[r, :, :, cols].reshape(2 * mine, head)
            q = pj[base : base + count, 2 * width + h * head : 2 * width + (h + 1) * head]
            s = lax.dot_general(q, keys, (((1,), (1,)), ((), ())), preferred_element_type=F32)
            if mask_row is None:
                t = jnp.concatenate(
                    [s[:rows] * mb[r, 0:1, :], s[rows:] * mb[r, 1:2, :]], axis=0
                )
            else:
                t = s * mb[r, mask_row : mask_row + 1, :]
            weights = silu_of_double(t).astype(BF16)
            acc[base : base + count, cols] += jnp.dot(weights, values, preferred_element_type=F32)

    arrived(hb, hb_recv)

    @pl.loop(0, ROUNDS)
    def _(r):
        give_own(r).start()
        xb[r, 0, slot_of(z), :] = hb[pl.ds(pl.multiple_of(r * part, part), part), :]

    w_copy.wait()
    project(hb, 0, rows)
    near_blocks(0)

    tri = lax.broadcasted_iota(jnp.int32, (rows, rows), 1) <= lax.broadcasted_iota(
        jnp.int32, (rows, rows), 0
    )
    for h in range(HEADS):
        cols = slice(h * head, (h + 1) * head)
        q = pj[0:rows, 2 * width + h * head : 2 * width + (h + 1) * head]
        k = pj[0:rows, 3 * width + h * head : 3 * width + (h + 1) * head]
        v = pj[0:rows, width + h * head : width + (h + 1) * head]
        s = lax.dot_general(q, k, (((1,), (1,)), ((), ())), preferred_element_type=F32)
        t = jnp.where(tri, s * half_scale, 0.0)
        acc[0:rows, cols] = jnp.dot(
            silu_of_double(t).astype(BF16), v, preferred_element_type=F32
        )

    arrived(cb, cb_recv)
    project(cb, rows, cands)
    near_blocks(1)
    for h in range(HEADS):
        cols = slice(h * head, (h + 1) * head)
        q = pj[rows:, 2 * width + h * head : 2 * width + (h + 1) * head].astype(F32)
        k = pj[rows:, 3 * width + h * head : 3 * width + (h + 1) * head].astype(F32)
        v = pj[rows:, width + h * head : width + (h + 1) * head].astype(F32)
        t = jnp.sum(q * k, axis=1, keepdims=True) * half_scale
        acc[rows:, cols] = silu_of_double(t).astype(BF16).astype(F32) * v
    far_block(0)
    arrived(mb, mb_recv)
    keys_values(0)

    arrived(ow_other, ow_recv.at[0])
    for copy in ow_second:
        copy.start()

    @pl.loop(1, ROUNDS)
    def _(r):
        @pl.when(r + 1 < ROUNDS)
        def _():
            near_blocks(r + 1)

        far_block(r)
        arrived(kv.at[r - 1, 1], d_recv.at[r - 1])
        attend(r - 1, 0, rows + cands, None)
        keys_values(r)

    for i in range(3):
        yy = lax.rem(y + 3 - i, 4)
        arrived(ow_from(zlo, yy), ow_recv.at[1 + i])
        arrived(ow_from(1 - zlo, yy), ow_recv.at[4 + i])
    ow_own.wait()
    ow_third.start()

    def finish(base, count):
        for j in range(base, base + count, 64):
            rows_of = slice(j, j + 64)
            gate = pj[rows_of, 0:width].astype(F32)
            gated[rows_of, :] = (layer_norm(acc[rows_of, :]) * gate).astype(BF16)

    last = ROUNDS - 1
    arrived(kv.at[last, 1], d_recv.at[last])
    attend(last, 0, rows, 0)
    finish(0, rows)
    arrived(ow.at[:, 1 - core], ow_recv.at[7])

    def branch(base, count, j):
        weight = ow[:, :, :, j : j + 256].reshape(width, 256)
        return jnp.dot(gated[base : base + count, :], weight, preferred_element_type=F32)

    for j in range(0, width, 256):
        mixed = hb[:, j : j + 256].astype(F32) + branch(0, rows, j)
        stage[:, j : j + 256] = mixed.astype(BF16)

    hist_back = remote(stage, hist_out.at[0], ret_send.at[0], ret_recv.at[0], swap)

    @pl.when(swapped == 1)
    def _():
        hist_back.start()

    @pl.when(swapped == 0)
    def _():
        pltpu.make_async_copy(stage, hist_out.at[0], ret_recv.at[0]).start()

    attend(last, rows, cands, 1)
    finish(rows, cands)
    for j in range(0, width, 256):
        mixed = cb[:, j : j + 256].astype(F32) + branch(rows, cands, j)
        cb[:, j : j + 256] = mixed.astype(BF16)
    lbuf[...] = lax.dot_general(
        task_t[...], cb[...], (((1,), (1,)), ((), ())), preferred_element_type=F32
    )
    logits_back = remote(lbuf, logits_out, ret_send.at[1], ret_recv.at[1], swap)

    @pl.when(swapped == 1)
    def _():
        logits_back.start()

    @pl.when(swapped == 0)
    def _():
        pltpu.make_async_copy(lbuf, logits_out, ret_recv.at[1]).start()

    @pl.loop(0, ROUNDS)
    def _(r):
        send_up(r).wait_send()
        send_down(r).wait_send()
        pass_up(r).wait_send()
        pass_down(r).wait_send()
        give_own(r).wait_send()
        give_down(r).wait_send()
        give_up(r).wait_send()
        give_far(r).wait_send()
        share(r).wait_send()

    for copy in (*ow_first, *ow_second, ow_third):
        copy.wait_send()

    @pl.when(swapped == 1)
    def _():
        hb_remote.wait_send()
        cb_remote.wait_send()
        mb_remote.wait_send()
        hist_back.wait_send()
        logits_back.wait_send()

    arrived(hist_out.at[0], ret_recv.at[0])
    arrived(logits_out, ret_recv.at[1])


def local(
    history, candidates, lengths, block_order, targets, projection, output_weight, task_weight
):
    rows, width = history.shape[1], history.shape[2]
    cands = candidates.shape[1]
    tasks = task_weight.shape[1]
    part = rows // ROUNDS
    mine = 8 * part
    any_space = pl.BlockSpec(memory_space=pl.ANY)
    smem = pl.BlockSpec(memory_space=pltpu.SMEM)
    vmem = pl.BlockSpec(memory_space=pltpu.VMEM)
    dma = pltpu.SemaphoreType.DMA
    hist_raw, logits = pl.pallas_call(
        kernel,
        out_shape=(
            jax.ShapeDtypeStruct((1, rows, width), BF16),
            jax.ShapeDtypeStruct((tasks, cands), F32),
        ),
        in_specs=[any_space, any_space, smem, smem, any_space, any_space, vmem],
        out_specs=(any_space, any_space),
        scratch_shapes=[
            pltpu.VMEM((width, 4 * width), BF16),
            pltpu.VMEM((8, 2, width // 16, width), BF16),
            pltpu.VMEM((rows, width), BF16),
            pltpu.VMEM((cands, width), BF16),
            pltpu.VMEM((ROUNDS, 2, 4 * part, width), BF16),
            pltpu.VMEM((ROUNDS, 2, mine, 2 * width), BF16),
            pltpu.VMEM((rows + cands, 4 * width), BF16),
            pltpu.VMEM((rows + cands, width), F32),
            pltpu.VMEM((rows + cands, width), BF16),
            pltpu.VMEM((rows, width), BF16),
            pltpu.VMEM((ROUNDS, 8, 2 * mine), F32),
            pltpu.VMEM((ROUNDS, 8, 2 * mine), F32),
            pltpu.VMEM((tasks, cands), F32),
            dma, dma, dma, dma, dma, dma, dma,
            dma((ROUNDS, 2)), dma((ROUNDS, 2)),
            dma((ROUNDS, 2)), dma((ROUNDS, 2)),
            dma((ROUNDS, 4)), dma((ROUNDS, 4)),
            dma((ROUNDS,)), dma((ROUNDS,)),
            dma((8,)), dma((8,)), dma,
            dma((2,)), dma((2,)),
        ],
        compiler_params=pltpu.CompilerParams(
            collective_id=0, has_side_effects=True, vmem_limit_bytes=56 * 2**20
        ),
    )(history, candidates, lengths, block_order, projection, output_weight, task_weight.T)
    own = block_order[0, lax.axis_index("ctx")]
    live = own * rows + jnp.arange(rows, dtype=jnp.int32) < lengths[0]
    layer_output = jnp.where(live[None, :, None], hist_raw, jnp.zeros_like(hist_raw))
    task_ids = jnp.arange(tasks, dtype=jnp.int32)
    picked = jnp.sum(jnp.where(targets[0][None, :] == task_ids[:, None], logits, 0.0), axis=0)
    return (layer_output, (-jax.nn.softplus(-picked))[None])


def solution(mesh):
    in_specs = (
        P("grp", "ctx", None),
        P("grp", "ctx", None),
        P("grp"),
        P("grp", None),
        P("grp", "ctx"),
        P(),
        P("grp", None),
        P(),
    )
    out_specs = (P("grp", "ctx", None), P("grp", "ctx"))
    return jax.shard_map(local, mesh=mesh, in_specs=in_specs, out_specs=out_specs, check_vma=False)
```

time: 267 us -> 94.6 us (0.35)
  waiting for transfers between devices: 195 us -> 0 us
  Pallas kernels: 0 us -> 88 us
  matrix products: 38.8 us -> 0 us
  between operations: 14.6 us -> 1.31 us
  local copies, waits for them, and re-layouts: 12.7 us -> 0.01 us
    all_gather x3 -> x0, waiting for transfers between devices: 194 us -> none  [the longest x1 90 us: local(): lax.all_gather(hist_keys, 'ctx', axis=0, tiled=True)]
    pallas_call x0 -> x1, Pallas kernels: none -> 88 us  [local(): pl.pallas_call(kernel, out_shape=(jax.ShapeDtypeStruct((1, rows, width),...]
    dot_general x5 -> x0, matrix products: 38.8 us -> none  [the longest x2 27 us: attend(): jnp.einsum('hqk,khd->qhd', weights, value_heads, preferred_element_type=j...]
    reshape x3 -> x0, local copies, waits for them, and re-layouts: 9.12 us -> none  [the longest x1 8.71 us: attend(): value_heads = values.reshape(key_rows, HEADS, -1)]
    unnamed x14 -> x2, local copies, waits for them, and re-layouts: 3.06 us -> 0.01 us
  transfers between devices with their start and end apart: 3 -> 0, of which waited for: 3 -> 0; matrix products, arithmetic and copies ran while one was open for 15% -> 0% of each run, Pallas kernels for 0% -> 0%
where the time goes in v1:
time: 94.6 us; the launch traced here: 94.4 us
  Pallas kernels  88 us (93%)
  other arithmetic  5.04 us (5%)
  between operations  1.31 us (1%)
    pallas_call x1, Pallas kernels, local(): pl.pallas_call(kernel, out_shape=(jax.ShapeDtypeStruct((1, rows, width),...  88 us

profile of v1, /device:TPU:1, one launch (start us, length us, event | category | flops | bytes accessed | tf_op | source)
XLA Modules:
  0.0 94.4 jit_solution(7722659188270635745)
XLA Ops:
  0.6 0.0 copy-start
  1.3 1.2 %fusion.1 = s32[1,1]{1,0:T(1,128)} fusion(s32[1,16]{1,0:T(1,128)} %order.1, s32[]{:T(128)S(6)} %select_n.22), kind=kLoop, calls=%fused_computation.7 | loop fusion | flops 1 | bytes 12 | tf_op jit(solution)/shard_map/mul | solution.py:423
  2.5 0.7 add_compare_fusion
  3.2 88.0 %shard_map.95 = (bf16[1,192,1024]{2,1,0:T(8,128)(2,1)}, f32[8,256]{1,0:T(8,128)}) custom-call(bf16[1,192,1024]{2,1,0:T(8,128)(2,1)} %hist.1, bf16[1,256,1024]{2,1,0:T(8,128)(2,1)} %cand.1, s32[1]{0:T(128)} %copy.10.lengths, s32[1,16]{1,0:T(1,128)} %order.1, bf16[1024,4096]{1,0:T(8,128)(2,1)} %proj.1, bf16[64,1024]{1,0:T(8,128)(2,1)} %out_weight.1, ...), custom_call_target="tpu_custom_call" | custom-call | tf_op jit(solution)/shard_map/pallas_call | solution.py:388
  91.2 1.8 %broadcast_select_fusion = bf16[1,192,1024]{2,1,0:T(8,128)(2,1)} fusion(bf16[1,192,1024]{2,1,0:T(8,128)(2,1)} %get-tuple-element.4, pred[192]{0:T(512)(128)(4,1)S(1)} %add_compare_fusion), kind=kLoop, calls=%fused_computation | loop fusion | flops 196608 | bytes 786624 | tf_op jit(solution)/shard_map/jit(_where)/select_n | solution.py:424
  93.0 0.0 copy-done
  93.0 0.7 select_reduce_fusion
  93.8 0.6 fusion
  (1 shorter events, 0.0 us)
Async XLA Ops:
  0.6 92.4 %copy-start = (s32[1,256]{1,0:T(1,128)S(1)}, s32[1,256]{1,0:T(1,128)}, u32[]{:S(2)}) copy-start(s32[1,256]{1,0:T(1,128)} %param.12) | copy-start | bytes 3076

commit v2 on v1

--- a/solution.py
+++ b/solution.py
@@ -10,6 +10,7 @@
 HEADS = 8
 NORM_EPS = 1e-05
 ROUNDS = 6
+AHEAD = 3
 F32, BF16 = jnp.float32, jnp.bfloat16
 MESH = pl.DeviceIdType.MESH
 
@@ -25,9 +26,9 @@
 
 
 def kernel(
-    hist, cand, lengths, order, proj, out_weight, task_t,
-    hist_out, logits_out,
-    w, ow, hb, cb, xb, kv, pj, acc, gated, stage, mloc, mb, lbuf,
+    hist, cand, lengths, order, targets, proj, out_weight, task_weight,
+    hist_out, logprob,
+    w, ow, hb, cb, xb, kv, pj, acc, gated, stage, mloc, mb, lbuf, lback, task_t,
     w_sem, hb_send, hb_recv, cb_send, cb_recv, mb_send, mb_recv,
     h_send, h_recv, z_send, z_recv, e_send, e_recv, d_send, d_recv,
     ow_send, ow_recv, ow_local, ret_send, ret_recv,
@@ -58,8 +59,6 @@
     z_far = lax.rem(z + 2, 4)
 
     swap = (pair + home_core, home_x * 4 + z)
-    home_up = (pair + home_core, home_x * 4 + z_up)
-    home_down = (pair + home_core, home_x * 4 + z_down)
     col_up = (g, x * 4 + z_up)
     col_down = (g, x * 4 + z_down)
     across = (g, (x + 1 - 2 * lax.rem(x, 2)) * 4 + z)
@@ -76,15 +75,13 @@
         pltpu.make_async_copy(ref, ref, sem).wait()
 
     barrier = pltpu.get_barrier_semaphore()
-    greeted = [home_up, home_down, across, sibling, z_pair, *y_others]
+    greeted = [col_up, col_down, across, sibling, z_pair, *y_others]
     for other in greeted:
         pl.semaphore_signal(barrier, inc=1, device_id=other, device_id_type=MESH)
 
     @pl.when(swapped == 1)
     def _():
         pl.semaphore_signal(barrier, inc=1, device_id=swap, device_id_type=MESH)
-        pl.semaphore_signal(barrier, inc=1, device_id=col_up, device_id_type=MESH)
-        pl.semaphore_signal(barrier, inc=1, device_id=col_down, device_id_type=MESH)
 
     w_copy = pltpu.make_async_copy(proj, w, w_sem)
     w_copy.start()
@@ -104,44 +101,37 @@
     row_id = lax.broadcasted_iota(jnp.int32, (8, 2 * mine), 0)
     first = block * rows + lax.rem(lane, part)
     causal = jnp.where(row_id == 0, block, -1) < own_block
+    own_live = (limit - own_block * rows).astype(F32)
+    task_t[...] = task_weight[...].astype(F32).T.astype(BF16)
     for r in range(ROUNDS):
         live = first + r * part < limit
-        mloc[r] = jnp.where(live & causal, half_scale, 0.0)
-
-    pl.semaphore_wait(barrier, len(greeted) + 3 * swapped)
-
-    def hist_part(r):
-        return hist.at[0, pl.ds(pl.multiple_of(r * part, part), part)]
+        mloc[r] = jnp.where(row_id == 2, own_live, jnp.where(live & causal, half_scale, 0.0))
+
+    pl.semaphore_wait(barrier, len(greeted) + swapped)
 
     def slot_of(zs):
         return pl.ds(pl.multiple_of(zs * part, part), part)
 
-    def send_up(r):
-        return remote(hist_part(r), xb.at[r, 0, slot_of(z)], h_send.at[r, 0], h_recv.at[r, 0], home_up)
-
-    def send_down(r):
-        return remote(hist_part(r), xb.at[r, 0, slot_of(z)], h_send.at[r, 1], h_recv.at[r, 1], home_down)
-
-    hb_remote = remote(hist.at[0], hb, hb_send, hb_recv, swap)
+    def part_of(r):
+        return pl.ds(pl.multiple_of(r * part, part), part)
+
+    def fetch_remote(r):
+        return remote(hist.at[0, part_of(r)], hb.at[part_of(r)], hb_send.at[r], hb_recv.at[r], swap)
+
     cb_remote = remote(cand.at[0], cb, cb_send, cb_recv, swap)
     mb_remote = remote(mloc, mb, mb_send, mb_recv, swap)
 
     @pl.when(swapped == 1)
     def _():
-        hb_remote.start()
-        cb_remote.start()
-        mb_remote.start()
+        for r in range(ROUNDS):
+            fetch_remote(r).start()
 
     @pl.when(swapped == 0)
     def _():
-        pltpu.make_async_copy(hist.at[0], hb, hb_recv).start()
+        for r in range(ROUNDS):
+            pltpu.make_async_copy(hist.at[0, part_of(r)], hb.at[part_of(r)], hb_recv.at[r]).start()
         pltpu.make_async_copy(cand.at[0], cb, cb_recv).start()
         pltpu.make_async_copy(mloc, mb, mb_recv).start()
-
-    @pl.loop(0, ROUNDS)
-    def _(r):
-        send_up(r).start()
-        send_down(r).start()
 
     ow_mine = out_weight
     ow_slot = ow.at[zlo * 4 + y, core]
@@ -161,7 +151,17 @@
     ow_third = remote(ow.at[:, core], ow.at[:, core], ow_send.at[7], ow_recv.at[7], sibling)
 
     def own_part(r):
-        return hb.at[pl.ds(pl.multiple_of(r * part, part), part)]
+        return hb.at[part_of(r)]
+
+    def send_up(r):
+        return remote(own_part(r), xb.at[r, 0, slot_of(z)], h_send.at[r, 0], h_recv.at[r, 0], col_up)
+
+    def send_down(r):
+        return remote(own_part(r), xb.at[r, 0, slot_of(z)], h_send.at[r, 1], h_recv.at[r, 1], col_down)
+
+    def send_own(r):
+        send_up(r).start()
+        send_down(r).start()
 
     def give(r, k, src, zs):
         return remote(src, xb.at[r, 1, slot_of(zs)], e_send.at[r, k], e_recv.at[r, k], across)
@@ -189,18 +189,48 @@
         ref = xb.at[r, 0, half_of(z_up, 1)]
         return remote(ref, ref, z_send.at[r, 1], z_recv.at[r, 1], col_down)
 
-    def near_blocks(r):
+    def up_near(r):
+        ref = xb.at[r, 1, slot_of(z)]
+        return remote(ref, ref, e_send.at[r, 1], e_recv.at[r, 1], col_up)
+
+    def down_near(r):
+        ref = xb.at[r, 1, slot_of(z)]
+        return remote(ref, ref, e_send.at[r, 2], e_recv.at[r, 2], col_down)
+
+    def up_far(r):
+        ref = xb.at[r, 1, half_of(z_down, 0)]
+        return remote(ref, ref, e_send.at[r, 3], e_recv.at[r, 3], col_up)
+
+    def down_far(r):
+        ref = xb.at[r, 1, half_of(z_up, 1)]
+        return remote(ref, ref, e_send.at[r, 4], e_recv.at[r, 4], col_down)
+
+    def near_blocks(r, across_too=True):
         arrived(xb.at[r, 0, slot_of(z_down)], h_recv.at[r, 0])
         pass_up(r).start()
-        give_down(r).start()
+        if across_too:
+            give_down(r).start()
         arrived(xb.at[r, 0, slot_of(z_up)], h_recv.at[r, 1])
         pass_down(r).start()
-        give_up(r).start()
-
-    def far_block(r):
+        if across_too:
+            give_up(r).start()
+
+    def far_block(r, across_too=True):
         arrived(xb.at[r, 0, half_of(z_far, 0)], z_recv.at[r, 0])
         arrived(xb.at[r, 0, half_of(z_far, 1)], z_recv.at[r, 1])
-        give_far(r).start()
+        if across_too:
+            give_far(r).start()
+
+    def near_across(r):
+        arrived(xb.at[r, 1, slot_of(z)], e_recv.at[r, 0])
+        up_near(r).start()
+        down_near(r).start()
+
+    def far_across(r):
+        arrived(xb.at[r, 1, slot_of(z_down)], e_recv.at[r, 1])
+        up_far(r).start()
+        arrived(xb.at[r, 1, slot_of(z_up)], e_recv.at[r, 2])
+        down_far(r).start()
 
     def share(r):
         return remote(kv.at[r, 0], kv.at[r, 1], d_send.at[r], d_recv.at[r], sibling)
@@ -210,9 +240,13 @@
             p = jnp.dot(src[...], w[:, j : j + 256], preferred_element_type=F32)
             pj[base : base + count, j : j + 256] = silu_of_double(0.5 * p).astype(BF16)
 
-    def keys_values(r):
-        for k, zs in enumerate((z, z_down, z_up, z_far)):
-            arrived(xb.at[r, 1, slot_of(zs)], e_recv.at[r, k])
+    def keys_values(r, across_too=True):
+        if across_too:
+            for k, zs in enumerate((z, z_down, z_up, z_far)):
+                arrived(xb.at[r, 1, slot_of(zs)], e_recv.at[r, k])
+        else:
+            for k in range(2):
+                arrived(xb.at[r, 1, half_of(z_far, k)], e_recv.at[r, 3 + k])
         block_rows = xb[r].reshape(mine, width)
         for j in range(0, 2 * width, 256):
             start = width + j if j < width else 2 * width + j
@@ -237,16 +271,23 @@
             weights = silu_of_double(t).astype(BF16)
             acc[base : base + count, cols] += jnp.dot(weights, values, preferred_element_type=F32)
 
-    arrived(hb, hb_recv)
-
-    @pl.loop(0, ROUNDS)
-    def _(r):
+    last = ROUNDS - 1
+    for r in range(ROUNDS):
+        arrived(own_part(r), hb_recv.at[r])
+        if r < AHEAD:
+            send_own(r)
         give_own(r).start()
-        xb[r, 0, slot_of(z), :] = hb[pl.ds(pl.multiple_of(r * part, part), part), :]
+        xb[r, 0, slot_of(z), :] = hb[r * part : (r + 1) * part, :]
+
+    @pl.when(swapped == 1)
+    def _():
+        cb_remote.start()
+        mb_remote.start()
 
     w_copy.wait()
     project(hb, 0, rows)
     near_blocks(0)
+    send_own(AHEAD)
 
     tri = lax.broadcasted_iota(jnp.int32, (rows, rows), 1) <= lax.broadcasted_iota(
         jnp.int32, (rows, rows), 0
@@ -262,9 +303,14 @@
             silu_of_double(t).astype(BF16), v, preferred_element_type=F32
         )
 
+    near_blocks(1)
+    send_own(AHEAD + 1)
+    far_block(0)
     arrived(cb, cb_recv)
     project(cb, rows, cands)
-    near_blocks(1)
+    near_blocks(2)
+    send_own(AHEAD + 2)
+    far_block(1)
     for h in range(HEADS):
         cols = slice(h * head, (h + 1) * head)
         q = pj[rows:, 2 * width + h * head : 2 * width + (h + 1) * head].astype(F32)
@@ -272,25 +318,39 @@
         v = pj[rows:, width + h * head : width + (h + 1) * head].astype(F32)
         t = jnp.sum(q * k, axis=1, keepdims=True) * half_scale
         acc[rows:, cols] = silu_of_double(t).astype(BF16).astype(F32) * v
-    far_block(0)
     arrived(mb, mb_recv)
     keys_values(0)
-
     arrived(ow_other, ow_recv.at[0])
     for copy in ow_second:
         copy.start()
 
-    @pl.loop(1, ROUNDS)
+    @pl.loop(1, last)
     def _(r):
-        @pl.when(r + 1 < ROUNDS)
+        @pl.when(r + 2 < last)
         def _():
-            near_blocks(r + 1)
-
-        far_block(r)
+            near_blocks(r + 2)
+
+        @pl.when(r + 2 == last)
+        def _():
+            near_blocks(last, False)
+            near_across(last)
+
+        @pl.when(r + 1 < last)
+        def _():
+            far_block(r + 1)
+
+        @pl.when(r + 1 == last)
+        def _():
+            far_block(last, False)
+            far_across(last)
+
+        keys_values(r)
         arrived(kv.at[r - 1, 1], d_recv.at[r - 1])
         attend(r - 1, 0, rows + cands, None)
-        keys_values(r)
-
+
+    keys_values(last, False)
+    arrived(kv.at[last - 1, 1], d_recv.at[last - 1])
+    attend(last - 1, 0, rows + cands, None)
     for i in range(3):
         yy = lax.rem(y + 3 - i, 4)
         arrived(ow_from(zlo, yy), ow_recv.at[1 + i])
@@ -304,7 +364,6 @@
             gate = pj[rows_of, 0:width].astype(F32)
             gated[rows_of, :] = (layer_norm(acc[rows_of, :]) * gate).astype(BF16)
 
-    last = ROUNDS - 1
     arrived(kv.at[last, 1], d_recv.at[last])
     attend(last, 0, rows, 0)
     finish(0, rows)
@@ -314,9 +373,10 @@
         weight = ow[:, :, :, j : j + 256].reshape(width, 256)
         return jnp.dot(gated[base : base + count, :], weight, preferred_element_type=F32)
 
+    row_live = lax.broadcasted_iota(jnp.int32, (rows, 256), 0).astype(F32) < mb[0, 2:3, 0:256]
     for j in range(0, width, 256):
         mixed = hb[:, j : j + 256].astype(F32) + branch(0, rows, j)
-        stage[:, j : j + 256] = mixed.astype(BF16)
+        stage[:, j : j + 256] = jnp.where(row_live, mixed, 0.0).astype(BF16)
 
     hist_back = remote(stage, hist_out.at[0], ret_send.at[0], ret_recv.at[0], swap)
 
@@ -336,7 +396,7 @@
     lbuf[...] = lax.dot_general(
         task_t[...], cb[...], (((1,), (1,)), ((), ())), preferred_element_type=F32
     )
-    logits_back = remote(lbuf, logits_out, ret_send.at[1], ret_recv.at[1], swap)
+    logits_back = remote(lbuf, lback, ret_send.at[1], ret_recv.at[1], swap)
 
     @pl.when(swapped == 1)
     def _():
@@ -344,7 +404,7 @@
 
     @pl.when(swapped == 0)
     def _():
-        pltpu.make_async_copy(lbuf, logits_out, ret_recv.at[1]).start()
+        pltpu.make_async_copy(lbuf, lback, ret_recv.at[1]).start()
 
     @pl.loop(0, ROUNDS)
     def _(r):
@@ -353,24 +413,36 @@
         pass_up(r).wait_send()
         pass_down(r).wait_send()
         give_own(r).wait_send()
-        give_down(r).wait_send()
-        give_up(r).wait_send()
-        give_far(r).wait_send()
         share(r).wait_send()
+
+        @pl.when(r < last)
+        def _():
+            give_down(r).wait_send()
+            give_up(r).wait_send()
+            give_far(r).wait_send()
+
+    up_near(last).wait_send()
+    down_near(last).wait_send()
+    up_far(last).wait_send()
+    down_far(last).wait_send()
 
     for copy in (*ow_first, *ow_second, ow_third):
         copy.wait_send()
 
     @pl.when(swapped == 1)
     def _():
-        hb_remote.wait_send()
+        for r in range(ROUNDS):
+            fetch_remote(r).wait_send()
         cb_remote.wait_send()
         mb_remote.wait_send()
         hist_back.wait_send()
         logits_back.wait_send()
 
+    arrived(lback, ret_recv.at[1])
+    task_id = lax.broadcasted_iota(jnp.int32, lback.shape, 0)
+    picked = jnp.sum(jnp.where(task_id == targets[...], lback[...], 0.0), axis=0, keepdims=True)
+    logprob[...] = jnp.minimum(picked, 0.0) - jnp.log1p(jnp.exp(-jnp.abs(picked)))
     arrived(hist_out.at[0], ret_recv.at[0])
-    arrived(logits_out, ret_recv.at[1])
 
 
 def local(
@@ -385,14 +457,14 @@
     smem = pl.BlockSpec(memory_space=pltpu.SMEM)
     vmem = pl.BlockSpec(memory_space=pltpu.VMEM)
     dma = pltpu.SemaphoreType.DMA
-    hist_raw, logits = pl.pallas_call(
+    return pl.pallas_call(
         kernel,
         out_shape=(
             jax.ShapeDtypeStruct((1, rows, width), BF16),
-            jax.ShapeDtypeStruct((tasks, cands), F32),
+            jax.ShapeDtypeStruct((1, cands), F32),
         ),
-        in_specs=[any_space, any_space, smem, smem, any_space, any_space, vmem],
-        out_specs=(any_space, any_space),
+        in_specs=[any_space, any_space, smem, smem, vmem, any_space, any_space, vmem],
+        out_specs=(any_space, vmem),
         scratch_shapes=[
             pltpu.VMEM((width, 4 * width), BF16),
             pltpu.VMEM((8, 2, width // 16, width), BF16),
@@ -407,10 +479,12 @@
             pltpu.VMEM((ROUNDS, 8, 2 * mine), F32),
             pltpu.VMEM((ROUNDS, 8, 2 * mine), F32),
             pltpu.VMEM((tasks, cands), F32),
-            dma, dma, dma, dma, dma, dma, dma,
+            pltpu.VMEM((tasks, cands), F32),
+            pltpu.VMEM((tasks, width), BF16),
+            dma, dma((ROUNDS,)), dma((ROUNDS,)), dma, dma, dma, dma,
             dma((ROUNDS, 2)), dma((ROUNDS, 2)),
             dma((ROUNDS, 2)), dma((ROUNDS, 2)),
-            dma((ROUNDS, 4)), dma((ROUNDS, 4)),
+            dma((ROUNDS, 5)), dma((ROUNDS, 5)),
             dma((ROUNDS,)), dma((ROUNDS,)),
             dma((8,)), dma((8,)), dma,
             dma((2,)), dma((2,)),
@@ -418,13 +492,7 @@
         compiler_params=pltpu.CompilerParams(
             collective_id=0, has_side_effects=True, vmem_limit_bytes=56 * 2**20
         ),
-    )(history, candidates, lengths, block_order, projection, output_weight, task_weight.T)
-    own = block_order[0, lax.axis_index("ctx")]
-    live = own * rows + jnp.arange(rows, dtype=jnp.int32) < lengths[0]
-    layer_output = jnp.where(live[None, :, None], hist_raw, jnp.zeros_like(hist_raw))
-    task_ids = jnp.arange(tasks, dtype=jnp.int32)
-    picked = jnp.sum(jnp.where(targets[0][None, :] == task_ids[:, None], logits, 0.0), axis=0)
-    return (layer_output, (-jax.nn.softplus(-picked))[None])
+    )(history, candidates, lengths, block_order, targets, projection, output_weight, task_weight)
 
 
 def solution(mesh):

time: 94.6 us -> 77.5 us (0.82)
  Pallas kernels: 88 us -> 71.5 us
  other arithmetic: 5.04 us -> 0 us
  local copies, waits for them, and re-layouts: 0.01 us -> 4.52 us
    pallas_call x1, Pallas kernels: 88 us -> 71.5 us  [local(): pl.pallas_call(kernel, out_shape=(jax.ShapeDtypeStruct((1, rows, width),...]
    unnamed x2 -> x3, local copies, waits for them, and re-layouts: 0.01 us -> 4.52 us
    select_n x1 -> x0, other arithmetic: 1.84 us -> none  [local(): jnp.where(live[None, :, None], hist_raw, jnp.zeros_like(hist_raw))]
    mul x1 -> x0, other arithmetic: 1.24 us -> none  [local(): live = own * rows + jnp.arange(rows, dtype=jnp.int32) < lengths[0]]
where the time goes in v2:
time: 77.5 us; the launch traced here: 77.3 us
  Pallas kernels  71.5 us (92%)
  local copies, waits for them, and re-layouts  4.52 us (6%)
  between operations  1.29 us (2%)
    pallas_call x1, Pallas kernels, local(): pl.pallas_call(kernel, out_shape=(jax.ShapeDtypeStruct((1, rows, width),...  71.5 us
    unnamed x3, local copies, waits for them, and re-layouts  4.52 us

profile of v2, /device:TPU:1, one launch (start us, length us, event | category | flops | bytes accessed | tf_op | source)
XLA Modules:
  0.0 77.3 jit_solution(11661192601732517713)
XLA Ops:
  1.3 1.6 %copy.10.task_weight = bf16[1024,8]{1,0:T(8,128)(2,1)} copy(bf16[1024,8]{0,1:T(8,128)(2,1)} %param.15) | data formatting | bytes 32768 | tf_op args[7]
  2.8 71.5 %shard_map.95 = (bf16[1,192,1024]{2,1,0:T(8,128)(2,1)}, f32[1,256]{1,0:T(1,128)}) custom-call(bf16[1,192,1024]{2,1,0:T(8,128)(2,1)} %hist.1, bf16[1,256,1024]{2,1,0:T(8,128)(2,1)} %cand.1, s32[1]{0:T(128)S(6)} %copy.13.lengths, s32[1,16]{1,0:T(1,128)} %order.1, s32[1,256]{1,0:T(1,128)} %targets.1, bf16[1024,4096]{1,0:T(8,128)(2,1)} %proj.1, ...), custom_call_target="tpu_custom_call" | custom-call | tf_op jit(solution)/shard_map/pallas_call | solution.py:460
  74.3 1.8 %copy.14 = bf16[1,192,1024]{2,1,0:T(8,128)(2,1)} copy(bf16[1,192,1024]{2,1,0:T(8,128)(2,1)} %get-tuple-element.4) | data formatting | bytes 786432
  76.1 1.2 %copy.15 = f32[1,256]{1,0:T(1,128)} copy(f32[1,256]{1,0:T(1,128)} %get-tuple-element.5) | data formatting | bytes 2048

commit v3 on v2

--- a/solution.py
+++ b/solution.py
@@ -10,7 +10,7 @@
 HEADS = 8
 NORM_EPS = 1e-05
 ROUNDS = 6
-AHEAD = 3
+AHEAD = 2
 F32, BF16 = jnp.float32, jnp.bfloat16
 MESH = pl.DeviceIdType.MESH
 
@@ -26,9 +26,9 @@
 
 
 def kernel(
-    hist, cand, lengths, order, targets, proj, out_weight, task_weight,
+    hist, cand, lengths, order, targets, proj, out_weight, task_t,
     hist_out, logprob,
-    w, ow, hb, cb, xb, kv, pj, acc, gated, stage, mloc, mb, lbuf, lback, task_t,
+    w, ow, hb, cb, xb, kv, pj, acc, gated, stage, mloc, mb, lbuf, lback,
     w_sem, hb_send, hb_recv, cb_send, cb_recv, mb_send, mb_recv,
     h_send, h_recv, z_send, z_recv, e_send, e_recv, d_send, d_recv,
     ow_send, ow_recv, ow_local, ret_send, ret_recv,
@@ -91,7 +91,7 @@
     lane = lax.broadcasted_iota(jnp.int32, (8, 2 * mine), 1)
     slot = lane // part
     own_block = order[0, c]
-    limit = lengths[0]
+    limit = lengths[0, 0]
     block = jnp.zeros_like(lane)
     x_pair = x + 1 - 2 * lax.rem(x, 2)
     columns = (x, x_pair, 3 - x, 3 - x_pair)
@@ -102,7 +102,6 @@
     first = block * rows + lax.rem(lane, part)
     causal = jnp.where(row_id == 0, block, -1) < own_block
     own_live = (limit - own_block * rows).astype(F32)
-    task_t[...] = task_weight[...].astype(F32).T.astype(BF16)
     for r in range(ROUNDS):
         live = first + r * part < limit
         mloc[r] = jnp.where(row_id == 2, own_live, jnp.where(live & causal, half_scale, 0.0))
@@ -329,6 +328,10 @@
         @pl.when(r + 2 < last)
         def _():
             near_blocks(r + 2)
+
+        @pl.when(r + 2 + AHEAD < ROUNDS)
+        def _():
+            send_own(r + 2 + AHEAD)
 
         @pl.when(r + 2 == last)
         def _():
@@ -480,7 +483,6 @@
             pltpu.VMEM((ROUNDS, 8, 2 * mine), F32),
             pltpu.VMEM((tasks, cands), F32),
             pltpu.VMEM((tasks, cands), F32),
-            pltpu.VMEM((tasks, width), BF16),
             dma, dma((ROUNDS,)), dma((ROUNDS,)), dma, dma, dma, dma,
             dma((ROUNDS, 2)), dma((ROUNDS, 2)),
             dma((ROUNDS, 2)), dma((ROUNDS, 2)),
@@ -492,7 +494,10 @@
         compiler_params=pltpu.CompilerParams(
             collective_id=0, has_side_effects=True, vmem_limit_bytes=56 * 2**20
         ),
-    )(history, candidates, lengths, block_order, targets, projection, output_weight, task_weight)
+    )(
+        history, candidates, lengths[None, :], block_order, targets, projection, output_weight,
+        task_weight.T,
+    )
 
 
 def solution(mesh):

time: 77.5 us -> 72.8 us (0.939)
  Pallas kernels: 71.5 us -> 68.3 us
  local copies, waits for them, and re-layouts: 4.52 us -> 2.96 us
    pallas_call x1, Pallas kernels: 71.5 us -> 68.3 us  [local(): pl.pallas_call(kernel, out_shape=(jax.ShapeDtypeStruct((1, rows, width),...]
    unnamed x3 -> x2, local copies, waits for them, and re-layouts: 4.52 us -> 2.96 us
where the time goes in v3:
time: 72.8 us; the launch traced here: 72.6 us
  Pallas kernels  68.3 us (94%)
  local copies, waits for them, and re-layouts  2.96 us (4%)
  between operations  1.29 us (2%)
    pallas_call x1, Pallas kernels, local(): pl.pallas_call(kernel, out_shape=(jax.ShapeDtypeStruct((1, rows, width),...  68.3 us
    unnamed x2, local copies, waits for them, and re-layouts  2.96 us

profile of v3, /device:TPU:1, one launch (start us, length us, event | category | flops | bytes accessed | tf_op | source)
XLA Modules:
  0.0 72.6 jit_solution(13298984642700572364)
XLA Ops:
  1.3 68.3 %shard_map.95 = (bf16[1,192,1024]{2,1,0:T(8,128)(2,1)}, f32[1,256]{1,0:T(1,128)}) custom-call(bf16[1,192,1024]{2,1,0:T(8,128)(2,1)} %hist.1, bf16[1,256,1024]{2,1,0:T(8,128)(2,1)} %cand.1, s32[1,1]{1,0:T(1,128)} %bitcast.2.lengths, s32[1,16]{1,0:T(1,128)} %order.1, s32[1,256]{1,0:T(1,128)} %targets.1, bf16[1024,4096]{1,0:T(8,128)(2,1)} %proj.1, ...), custom_call_target="tpu_custom_call" | custom-call | tf_op jit(solution)/shard_map/pallas_call | solution.py:463
  69.6 1.8 %copy.13 = bf16[1,192,1024]{2,1,0:T(8,128)(2,1)} copy(bf16[1,192,1024]{2,1,0:T(8,128)(2,1)} %get-tuple-element.4) | data formatting | bytes 786432
  71.4 1.2 %copy.14 = f32[1,256]{1,0:T(1,128)} copy(f32[1,256]{1,0:T(1,128)} %get-tuple-element.5) | data formatting | bytes 2048

commit v4 on v3

--- a/solution.py
+++ b/solution.py
@@ -305,11 +305,12 @@
     near_blocks(1)
     send_own(AHEAD + 1)
     far_block(0)
-    arrived(cb, cb_recv)
-    project(cb, rows, cands)
     near_blocks(2)
     send_own(AHEAD + 2)
     far_block(1)
+    keys_values(0)
+    arrived(cb, cb_recv)
+    project(cb, rows, cands)
     for h in range(HEADS):
         cols = slice(h * head, (h + 1) * head)
         q = pj[rows:, 2 * width + h * head : 2 * width + (h + 1) * head].astype(F32)
@@ -318,7 +319,6 @@
         t = jnp.sum(q * k, axis=1, keepdims=True) * half_scale
         acc[rows:, cols] = silu_of_double(t).astype(BF16).astype(F32) * v
     arrived(mb, mb_recv)
-    keys_values(0)
     arrived(ow_other, ow_recv.at[0])
     for copy in ow_second:
         copy.start()

time: 72.8 us -> 74 us (1.016)
  Pallas kernels: 68.3 us -> 69.5 us
    pallas_call x1, Pallas kernels: 68.3 us -> 69.5 us  [local(): pl.pallas_call(kernel, out_shape=(jax.ShapeDtypeStruct((1, rows, width),...]
where the time goes in v4:
time: 74 us; the launch traced here: 73.8 us
  Pallas kernels  69.5 us (94%)
  local copies, waits for them, and re-layouts  2.96 us (4%)
  between operations  1.29 us (2%)
    pallas_call x1, Pallas kernels, local(): pl.pallas_call(kernel, out_shape=(jax.ShapeDtypeStruct((1, rows, width),...  69.5 us
    unnamed x2, local copies, waits for them, and re-layouts  2.96 us

profile of v4, /device:TPU:1, one launch (start us, length us, event | category | flops | bytes accessed | tf_op | source)
XLA Modules:
  0.0 73.8 jit_solution(652652271548974865)
XLA Ops:
  1.3 69.5 %shard_map.95 = (bf16[1,192,1024]{2,1,0:T(8,128)(2,1)}, f32[1,256]{1,0:T(1,128)}) custom-call(bf16[1,192,1024]{2,1,0:T(8,128)(2,1)} %hist.1, bf16[1,256,1024]{2,1,0:T(8,128)(2,1)} %cand.1, s32[1,1]{1,0:T(1,128)} %bitcast.2.lengths, s32[1,16]{1,0:T(1,128)} %order.1, s32[1,256]{1,0:T(1,128)} %targets.1, bf16[1024,4096]{1,0:T(8,128)(2,1)} %proj.1, ...), custom_call_target="tpu_custom_call" | custom-call | tf_op jit(solution)/shard_map/pallas_call | solution.py:463
  70.8 1.8 %copy.13 = bf16[1,192,1024]{2,1,0:T(8,128)(2,1)} copy(bf16[1,192,1024]{2,1,0:T(8,128)(2,1)} %get-tuple-element.4) | data formatting | bytes 786432
  72.6 1.2 %copy.14 = f32[1,256]{1,0:T(1,128)} copy(f32[1,256]{1,0:T(1,128)} %get-tuple-element.5) | data formatting | bytes 2048
